TPU v7x, 512 devices: a whole 4x8x8 slice. The times are simulated.
512 devices in a mesh: seq: 32 (over x, z), chan: 16 (over y, core).
Axes of the slice: x: 4, y: 8, z: 8, core: 2. Of those that a mesh axis runs over, the one named last changes fastest.
Arguments:
- query_gate: bfloat16 [16384, 8192], P('seq', 'chan'), may hold values from -23 to 23
- key_gate: bfloat16 [16384, 8192], P('seq', 'chan'), may hold values from -6 to 6
- value_input: bfloat16 [16384, 8192], P('seq', 'chan'), may hold values from -6 to 6
- filter_taps: bfloat16 [16384, 128], P('seq', 'chan'), may hold values from -1 to 1
- norm_gain: float32 [8192], P('chan'), may hold values from 0.5 to 1.5
Outputs:
- gated: bfloat16 [16384, 8192], P('seq', 'chan')
- normed: bfloat16 [16384, 8192], P('seq', 'chan')
All inputs are finite; a program needn't handle non-finite values.
Results may differ from a plain program's by a relative error of at most 0.01.
Values may be sent and summed in bfloat16 or wider, within the bound.
A program may use at most 64 MiB of HBM per device.

v0:
```python
import math

import jax
import jax.numpy as jnp
from jax import lax
from jax.sharding import PartitionSpec as P

D = 8192
GROUPS = 128


norm_eps = 1e-05


def from_everyone(value, axis):
    copies = jnp.broadcast_to(value, (lax.axis_size(axis), *value.shape))
    return lax.all_to_all(copies, axis, split_axis=0, concat_axis=0, tiled=True)


def over_copies(value, axis):
    return from_everyone(value, axis).sum(axis=0)


def angle_table(rows_count, cols_count, period):
    row_ids = lax.iota(jnp.int32, rows_count)
    col_ids = lax.iota(jnp.int32, cols_count)
    phases = row_ids[:, None] * col_ids[None, :] % period
    return phases.astype(jnp.float32) * (2.0 * math.pi / period)


def block_matrix(rows_count, cols_count, period):
    phases = angle_table(rows_count, cols_count, period)
    return jnp.stack([jnp.cos(phases), -jnp.sin(phases)]).astype(jnp.bfloat16)


def line_matrix(length, direction):
    phases = angle_table(length, length, length)
    cosine = jnp.cos(phases)
    sine_part = jnp.sin(phases) * direction
    upper = jnp.concatenate([cosine, sine_part], axis=1)
    lower = jnp.concatenate([-sine_part, cosine], axis=1)
    return jnp.concatenate([upper, lower], axis=0).astype(jnp.bfloat16)


def twiddle_minor(real_in, imag_in, period, direction):
    phases = angle_table(real_in.shape[1], real_in.shape[2], period)
    cosine = jnp.cos(phases)[None, :, :]
    sine_part = direction * jnp.sin(phases)[None, :, :]
    real_part = real_in * cosine - imag_in * sine_part
    imaginary = imag_in * cosine + real_in * sine_part
    return (real_part, imaginary)


def spectrum_minor(rows_in, first_matrix, right_forward, periods):
    spread = jnp.einsum("cab,rak->rckb", rows_in, first_matrix, preferred_element_type=jnp.float32)
    real_part, imaginary = twiddle_minor(spread[0], spread[1], periods, -1.0)
    joined = jnp.concatenate(
        [real_part.astype(jnp.bfloat16), imaginary.astype(jnp.bfloat16)], axis=2
    )
    return jnp.einsum("ckb,bm->ckm", joined, right_forward, preferred_element_type=jnp.float32)


def body(query_gate, key_gate, value_input, filter_taps, norm_gain):
    tokens, channels = key_gate.shape
    blocks = lax.axis_size("seq")
    periods = 2 * tokens * blocks
    product = (key_gate.astype(jnp.float32) * value_input.astype(jnp.float32)).astype(jnp.bfloat16)
    first_matrix = block_matrix(blocks, 2 * blocks, 2 * blocks)
    last_matrix = block_matrix(2 * blocks, blocks, 2 * blocks)
    line_forward = line_matrix(tokens, 1.0)
    line_backward = line_matrix(tokens, -1.0)
    width_here = channels // blocks
    group_width = D // GROUPS
    repeat_count = max(1, group_width // width_here)
    taps_wide = jnp.repeat(filter_taps, repeat_count, axis=1)
    data_major = jnp.transpose(product)
    taps_major = jnp.transpose(taps_wide)
    data_whole, taps_whole = (
        lax.all_to_all(data_major, "seq", split_axis=0, concat_axis=1, tiled=True),
        lax.all_to_all(taps_major, "seq", split_axis=0, concat_axis=1, tiled=True),
    )
    taps_cols = taps_whole.shape[0]
    data_rows = data_whole.reshape(width_here, blocks, tokens)
    taps_rows = taps_whole.reshape(taps_cols, blocks, tokens)
    right_forward = jnp.transpose(line_forward)
    right_backward = jnp.transpose(line_backward)
    spectrum = spectrum_minor(data_rows, first_matrix, right_forward, periods)
    taps_spectrum = spectrum_minor(taps_rows, first_matrix, right_forward, periods)
    grouped = spectrum.reshape(taps_cols, width_here // taps_cols, 2 * blocks, 2 * tokens)
    spec_real = grouped[..., :tokens]
    spec_imag = grouped[..., tokens:]
    filter_real = taps_spectrum[:, None, :, :tokens]
    filter_imag = taps_spectrum[:, None, :, tokens:]
    filtered_real = (spec_real * filter_real - spec_imag * filter_imag).astype(jnp.bfloat16)
    filtered_imag = (spec_real * filter_imag + spec_imag * filter_real).astype(jnp.bfloat16)
    filtered = jnp.concatenate([filtered_real, filtered_imag], axis=3).reshape(
        width_here, 2 * blocks, 2 * tokens
    )
    inverted = jnp.einsum(
        "ckm,mb->ckb", filtered, right_backward, preferred_element_type=jnp.float32
    )
    back_real, back_imag = twiddle_minor(
        inverted[..., :tokens], inverted[..., tokens:], periods, 1.0
    )
    returned = jnp.stack([back_real, back_imag]).astype(jnp.bfloat16)
    summed = jnp.einsum("rckb,rka->cab", returned, last_matrix, preferred_element_type=jnp.float32)
    local_blocks = (
        (summed * (1.0 / periods)).astype(jnp.bfloat16).reshape(width_here, blocks * tokens)
    )
    convolved_major = lax.all_to_all(local_blocks, "seq", split_axis=1, concat_axis=0, tiled=True)
    convolved = jnp.transpose(convolved_major)
    gated_full = query_gate.astype(jnp.float32) * convolved.astype(jnp.float32)
    partial_squares = jnp.sum(gated_full * gated_full, axis=1)
    square_sum = over_copies(partial_squares, "chan")
    inverse_rms = lax.rsqrt(square_sum / D + norm_eps)
    normed = gated_full * inverse_rms[:, None] * norm_gain[None, :]
    return (gated_full.astype(jnp.bfloat16), normed.astype(jnp.bfloat16))


def solution(mesh):
    placed = (P("seq", "chan"), P("seq", "chan"), P("seq", "chan"), P("seq", "chan"), P("chan"))
    return jax.shard_map(
        body,
        mesh=mesh,
        in_specs=placed,
        out_specs=(P("seq", "chan"), P("seq", "chan")),
        check_vma=False,
    )
```

profile of v0, /device:TPU:1, one launch (start us, length us, event | category | flops | bytes accessed | tf_op | source)
XLA Modules:
  0.0 104.3 jit_solution(1919968951867319143)
XLA Ops:
  0.6 0.0 copy-start
  0.6 0.0 copy-start.1
  0.7 0.8 broadcast_in_dim.4
  1.5 0.5 broadcast.409
  2.0 0.7 reduce.1
  2.6 0.6 reshape.300
  3.3 13.8 %all-to-all-start.1 = ((bf16[32,2,256]{2,1,0:T(2,128)(2,1)}), bf16[32,2,256]{2,1,0:T(2,128)(2,1)}, u32[]{:S(2)}, u32[]{:S(2)}) async-start(bf16[32,2,256]{2,1,0:T(2,128)(2,1)} %reshape.300), calls=%async_computation.1 | async-start | bytes 65536 | tf_op jit(solution)/shard_map/all_to_all | solution.py:80
  17.1 0.5 broadcast_multiply_fusion
  17.7 5.2 %negate_convert_fusion.1 = (bf16[512,512]{1,0:T(8,128)(2,1)}, bf16[512,512]{1,0:T(8,128)(2,1)S(1)}) fusion(), kind=kLoop, calls=%fused_computation.48 | loop fusion | flops 4456448 | bytes 1048576 | tf_op jit(solution)/shard_map/convert.15
  22.9 4.0 %negate_convert_fusion = (bf16[512,512]{1,0:T(8,128)(2,1)S(1)}, bf16[512,512]{1,0:T(8,128)(2,1)S(1)}) fusion(), kind=kLoop, calls=%fused_computation.47 | loop fusion | flops 4718592 | bytes 1048576 | tf_op jit(solution)/shard_map/convert.9
  26.9 0.5 fusion.59
  27.4 0.0 copy-done
  27.4 0.2 copy.43
  27.6 0.0 copy-done.1
  27.6 0.2 copy.44
  27.9 0.0 copy-start.3
  27.9 0.9 multiply_convert_fusion.1
  28.8 0.1 negate_convert_fusion.2
  28.9 0.0 all-to-all-done.1
  28.9 9.3 %all-to-all-start = ((bf16[32,16,512]{2,1,0:T(8,128)(2,1)}), bf16[32,16,512]{2,1,0:T(8,128)(2,1)S(1)}, u32[]{:S(2)}, u32[]{:S(2)}) async-start(bf16[32,16,512]{2,1,0:T(8,128)(2,1)} %bitcast.4), calls=%async_computation | async-start | bytes 1048576 | tf_op jit(solution)/shard_map/all_to_all | solution.py:79
  38.2 0.7 negate_convert_fusion.3
  38.9 4.6 %fusion.42 = bf16[512,512]{1,0:T(8,128)(2,1)} fusion(), kind=kLoop, calls=%fused_computation.58 | loop fusion | flops 3932160 | bytes 524288 | tf_op jit(solution)/shard_map/convert.18
  43.5 0.8 reshape.301
  44.3 0.2 fusion.61
  44.5 0.6 subtract_convert_fusion.3
  45.1 0.0 copy-done.3
  45.1 1.8 %convolution_bitcast_fusion.2 = f32[1,64,1024]{2,1,0:T(8,128)S(1)} fusion(bf16[512,512]{1,0:T(8,128)(2,1)S(1)} %get-tuple-element.29, bf16[512,512]{1,0:T(8,128)(2,1)S(1)} %copy-done.3, bf16[512,512]{1,0:T(8,128)(2,1)} %fusion.42, bf16[1,64,512]{2,1,0:T(8,128)(2,1)S(1)} %get-tuple-element.23, bf16[1,64,512]{2,1,0:T(8,128)(2,1)S(1)} %get-tuple-element.22), kind=kOutput, calls=%fused_computation.38 | convolution fusion | flops 142868480 | bytes 1966080 | tf_op jit(solution)/shard_map/ckb,bm->ckm/dot_general | solution.py:60
  46.9 4.9 %all-to-all-done = bf16[32,16,512]{2,1,0:T(8,128)(2,1)S(1)} async-done(((bf16[32,16,512]{2,1,0:T(8,128)(2,1)}), bf16[32,16,512]{2,1,0:T(8,128)(2,1)S(1)}, u32[]{:S(2)}, u32[]{:S(2)}) %all-to-all-start) | async-done | bytes 524320 | tf_op jit(solution)/shard_map/all_to_all | solution.py:79
  51.8 0.7 convolution_bitcast_fusion.1
  52.5 0.0 copy-start.4
  52.5 0.7 subtract_convert_fusion.2
  53.3 0.3 copy-done.4
  53.6 2.4 %convolution_bitcast_fusion = f32[1,16,64,1024]{3,2,1,0:T(8,128)S(1)} fusion(bf16[16,64,512]{2,1,0:T(8,128)(2,1)S(1)} %get-tuple-element.17, bf16[16,64,512]{2,1,0:T(8,128)(2,1)S(1)} %get-tuple-element.16, bf16[512,512]{1,0:T(8,128)(2,1)S(1)} %get-tuple-element.29, bf16[512,512]{1,0:T(8,128)(2,1)S(1)} %copy-done.3, bf16[512,512]{1,0:T(8,128)(2,1)S(1)} %copy-done.4), kind=kOutput, calls=%fused_computation.4 | convolution fusion | flops 2160066560 | bytes 7864320 | tf_op jit(solution)/shard_map/ckb,bm->ckm/dot_general | solution.py:60
  55.9 0.7 subtract_convert_fusion.1
  56.6 2.4 %fusion.3 = f32[16,64,1024]{2,1,0:T(8,128)S(1)} fusion(bf16[512,512]{1,0:T(8,128)(2,1)S(1)} %get-tuple-element.29, bf16[1,16,64,512]{3,2,1,0:T(8,128)(2,1)S(1)} %get-tuple-element.15, bf16[1,16,64,512]{3,2,1,0:T(8,128)(2,1)S(1)} %get-tuple-element.14, bf16[512,512]{1,0:T(8,128)(2,1)S(1)} %get-tuple-element.30, bf16[512,512]{1,0:T(8,128)(2,1)S(1)} %get-tuple-element.31), kind=kOutput, calls=%fused_computation.9 | convolution fusion | flops 2160066560 | bytes 7864320 | tf_op jit(solution)/shard_map/ckm,mb->ckb/dot_general | solution.py:99
  59.0 0.0 copy-start.5
  59.0 0.0 copy-start.6
  59.0 0.7 fusion.32
  59.7 0.0 copy-done.5
  59.7 0.0 copy-done.6
  59.7 0.0 copy-start.2
  59.7 0.5 fusion.26
  60.2 0.0 copy-start.7
  60.2 1.1 %copy.48 = bf16[16,32,512]{2,0,1:T(8,128)(2,1)} copy(bf16[16,32,512]{2,1,0:T(8,128)(2,1)S(1)} %fusion.26) | data formatting | bytes 1048576 | tf_op jit(solution)/shard_map/convert_element_type | solution.py:108
  61.3 7.9 %all-to-all-start.2 = ((bf16[16,32,512]{2,0,1:T(8,128)(2,1)}), bf16[16,32,512]{2,0,1:T(8,128)(2,1)S(1)}, u32[]{:S(2)}, u32[]{:S(2)}) async-start(bf16[16,32,512]{2,0,1:T(8,128)(2,1)} %copy.48), calls=%async_computation.2 | async-start | bytes 1048576 | tf_op jit(solution)/shard_map/all_to_all | solution.py:110
  69.2 0.0 copy-done.2
  69.2 0.2 copy.42
  69.4 12.7 %all-to-all-done.2 = bf16[16,32,512]{2,0,1:T(8,128)(2,1)S(1)} async-done(((bf16[16,32,512]{2,0,1:T(8,128)(2,1)}), bf16[16,32,512]{2,0,1:T(8,128)(2,1)S(1)}, u32[]{:S(2)}, u32[]{:S(2)}) %all-to-all-start.2) | async-done | bytes 524320 | tf_op jit(solution)/shard_map/all_to_all | solution.py:110
  82.1 0.2 multiply_reduce_fusion
  82.4 19.7 %all_to_all.48 = f32[16,1,512]{2,1,0:T(1,128)S(1)} all-to-all(f32[16,1,512]{2,1,0:T(1,128)S(1)} %broadcast_in_dim.5), channel_id=1, replica_groups=mesh['seq'=32,'chan'=16] {'chan'}, dimensions={0} | all-to-all | bytes 65536 | tf_op jit(solution)/shard_map/all_to_all | solution.py:17
  102.1 0.0 copy-done.7
  102.1 0.2 multiply_convert_fusion
  102.3 1.0 copy.50
  103.3 1.0 copy.51
  (5 shorter events, 0.1 us)
Async XLA Ops:
  0.6 26.8 %copy-start = (bf16[512,512]{1,0:T(8,128)(2,1)S(1)}, bf16[512,512]{1,0:T(8,128)(2,1)}, u32[]{:S(2)}) copy-start(bf16[512,512]{1,0:T(8,128)(2,1)} %param.6) | copy-start | bytes 1572868
  0.6 27.0 %copy-start.1 = (bf16[512,512]{1,0:T(8,128)(2,1)S(1)}, bf16[512,512]{1,0:T(8,128)(2,1)}, u32[]{:S(2)}) copy-start(bf16[512,512]{1,0:T(8,128)(2,1)} %param.7) | copy-start | bytes 1572868
  3.3 25.6 %all-to-all-start.1 = ((bf16[32,2,256]{2,1,0:T(2,128)(2,1)}), bf16[32,2,256]{2,1,0:T(2,128)(2,1)}, u32[]{:S(2)}, u32[]{:S(2)}) async-start(bf16[32,2,256]{2,1,0:T(2,128)(2,1)} %reshape.300), calls=%async_computation.1 | async-start | bytes 65536 | tf_op jit(solution)/shard_map/all_to_all | solution.py:80
  27.9 17.3 %copy-start.3 = (bf16[512,512]{1,0:T(8,128)(2,1)S(1)}, bf16[512,512]{1,0:T(8,128)(2,1)}, u32[]{:S(2)}) copy-start(bf16[512,512]{1,0:T(8,128)(2,1)} %get-tuple-element.28) | copy-start | bytes 1572868
  28.9 22.9 %all-to-all-start = ((bf16[32,16,512]{2,1,0:T(8,128)(2,1)}), bf16[32,16,512]{2,1,0:T(8,128)(2,1)S(1)}, u32[]{:S(2)}, u32[]{:S(2)}) async-start(bf16[32,16,512]{2,1,0:T(8,128)(2,1)} %bitcast.4), calls=%async_computation | async-start | bytes 1048576 | tf_op jit(solution)/shard_map/all_to_all | solution.py:79
  52.5 1.0 %copy-start.4 = (bf16[512,512]{1,0:T(8,128)(2,1)S(1)}, bf16[512,512]{1,0:T(8,128)(2,1)}, u32[]{:S(2)}) copy-start(bf16[512,512]{1,0:T(8,128)(2,1)} %fusion.42) | copy-start | bytes 1572868
  59.0 0.7 copy-start.5
  59.0 0.7 copy-start.6
  59.7 9.5 %copy-start.2 = (bf16[512,512]{1,0:T(8,128)(2,1)S(1)}, bf16[512,512]{1,0:T(8,128)(2,1)}, u32[]{:S(2)}) copy-start(bf16[512,512]{1,0:T(8,128)(2,1)} %param.5) | copy-start | bytes 1572868
  60.2 41.9 %copy-start.7 = (f32[512]{0:T(512)S(1)}, f32[512]{0:T(512)}, u32[]{:S(2)}) copy-start(f32[512]{0:T(512)} %param.9) | copy-start | bytes 6148
  61.3 20.9 %all-to-all-start.2 = ((bf16[16,32,512]{2,0,1:T(8,128)(2,1)}), bf16[16,32,512]{2,0,1:T(8,128)(2,1)S(1)}, u32[]{:S(2)}, u32[]{:S(2)}) async-start(bf16[16,32,512]{2,0,1:T(8,128)(2,1)} %copy.48), calls=%async_computation.2 | async-start | bytes 1048576 | tf_op jit(solution)/shard_map/all_to_all | solution.py:110
where the time goes:
time: 105 us; the launch traced here: 104 us
  starting transfers between devices  31.1 us (30%)
  other arithmetic  20.4 us (19%)
  blocking collectives  19.7 us (19%)
  waiting for transfers between devices  17.6 us (17%)
  matrix products  7.9 us (8%)
  local copies, waits for them, and re-layouts  6.83 us (7%)
    all_to_all x1, blocking collectives, from_everyone(): return lax.all_to_all(copies, axis, split_axis=0, concat_axis=0, tiled=True)  19.7 us
    another operation x5, other arithmetic  14.6 us
    all_to_all x1, starting transfers between devices, body(): lax.all_to_all(taps_major, 'seq', split_axis=0, concat_axis=1, tiled=True)  13.8 us
    all_to_all x1, waiting for transfers between devices, body(): lax.all_to_all(local_blocks, 'seq', split_axis=1, concat_axis=0, tiled=True)  12.7 us
    all_to_all x1, starting transfers between devices, body(): lax.all_to_all(data_major, 'seq', split_axis=0, concat_axis=1, tiled=True)  9.34 us
    all_to_all x1, starting transfers between devices, body(): lax.all_to_all(local_blocks, 'seq', split_axis=1, concat_axis=0, tiled=True)  7.92 us
    all_to_all x1, waiting for transfers between devices, body(): lax.all_to_all(data_major, 'seq', split_axis=0, concat_axis=1, tiled=True)  4.86 us
    unnamed x23, local copies, waits for them, and re-layouts  4.38 us
  transfers between devices with their start and end apart: 3, of which 2 were waited for; matrix products, arithmetic and copies ran while one was open for 20% of the time, Pallas kernels for 0%

commit v1 on v0

v1 whole, which is shorter than its diff:
```python
import functools

import jax
import jax.numpy as jnp
import ml_dtypes
import numpy as np
from jax import lax
from jax.experimental import pallas as pl
from jax.experimental.pallas import tpu as pltpu
from jax.sharding import PartitionSpec as P

D = 8192
GROUPS = 128
NORM_EPS = 1e-05
MESH = pl.DeviceIdType.MESH

X_DIM, Z_DIM = 4, 8
SEQ = X_DIM * Z_DIM
CHAN = 16
TOK = 512
CH = 512
CW = CH // SEQ
LINES = 2 * SEQ
HALF = LINES // 2 + 1
N = 2 * SEQ * TOK
FULL = LINES * CW
PARTS = 2
CP = CW // PARTS
BH = TOK // 2
ROWS = HALF * CP + CP
TPAD = 48


def rounded(values):
    return values.astype(np.float32).astype(ml_dtypes.bfloat16)


def constant_tables():
    k1 = np.arange(HALF)
    a = np.arange(SEQ)
    b = np.arange(TOK)
    ang = 2.0 * np.pi * ((k1[:, None] * a[None, :]) % LINES) / LINES
    cos_a, sin_a = np.cos(ang), np.sin(ang)
    eye = np.eye(CW)
    first = np.concatenate([cos_a, -sin_a[1:-1]], axis=0)
    first_kron = np.kron(first, eye)
    weight = np.full((HALF, 1), 2.0)
    weight[0] = weight[-1] = 1.0
    last = np.concatenate([weight * cos_a, -2.0 * sin_a[1:-1]], axis=0)
    last_kron = np.kron(last.T, eye)
    taps_first = np.zeros((2, TPAD, SEQ))
    taps_first[0, :HALF] = cos_a
    taps_first[1, 1 : HALF - 1] = -sin_a[1:-1]
    taps_first = taps_first.reshape(2 * TPAD, SEQ)
    tang = 2.0 * np.pi * ((k1[:, None] * b[None, :]) % N) / N
    twiddle = np.zeros((2, TPAD, TOK))
    twiddle[0, :HALF], twiddle[1, :HALF] = np.cos(tang), np.sin(tang)
    lang = 2.0 * np.pi * ((b[:, None] * b[None, :]) % TOK) / TOK
    c, s = np.cos(lang), np.sin(lang)
    forward = np.block([[c, -s], [s, c]])
    backward = np.block([[c, s], [-s, c]])
    order = np.concatenate(
        [np.concatenate([np.arange(128) + 128 * i, np.arange(128) + 128 * i + TOK]) for i in range(TOK // 128)]
    )
    forward = forward[:, order]
    backward = backward[order][:, order]
    pairs = np.concatenate([np.arange(256) + 256 * i for i in (0, 2, 1, 3)])
    backward = backward[:, pairs]
    return (
        rounded(first_kron),
        rounded(last_kron),
        rounded(taps_first),
        twiddle.astype(np.float32),
        rounded(forward),
        rounded(backward),
    )


def send_order():
    zs = (4, 3, 5, 2, 6, 1, 7, 0)
    out = []
    for k in range(Z_DIM):
        for dx in range(X_DIM):
            dz = zs[(k + 2 * dx) % Z_DIM]
            if (dx, dz) != (0, 0):
                out.append((dx, dz))
    return out


def kernel(
    q_hbm, k_hbm, v_hbm, taps_hbm, first_hbm, last_hbm, tfirst_hbm, twid_hbm, fwd_hbm, bwd_hbm,
    conv_ref, inverse_ref,
    q_ref, k_ref, v_ref, taps_ref, tfirst_ref, twid_ref,
    prod_t, data_in, taps_out, taps_in, taps_mat, taps_spec, q_t,
    first, last, fwd, bwd, spread, filtered, returned, back_out, back_in, conv, inverse_wide, sums_out, sums_in,
    load_sem, data_ssem, data_rsem, taps_ssem, taps_rsem, back_ssem, back_rsem, sum_ssem, sum_rsem,
):
    f32, bf16 = jnp.float32, jnp.bfloat16
    me = lax.axis_index("seq")
    ch = lax.axis_index("chan")
    my_x, my_z = me // Z_DIM, me % Z_DIM

    loads = [
        (k_hbm, k_ref), (v_hbm, v_ref), (taps_hbm, taps_ref), (q_hbm, q_ref), (tfirst_hbm, tfirst_ref),
        (twid_hbm, twid_ref), (fwd_hbm, fwd), (first_hbm, first), (bwd_hbm, bwd), (last_hbm, last),
    ]
    loads = [pltpu.make_async_copy(src, dst, load_sem.at[i]) for i, (src, dst) in enumerate(loads)]
    for load in loads:
        load.start()

    def peer(dx, dz):
        return lax.rem(my_x + dx, X_DIM) * Z_DIM + lax.rem(my_z + dz, Z_DIM)

    order = send_order()
    barrier = pltpu.get_barrier_semaphore()
    for dx, dz in order:
        pl.semaphore_signal(barrier, inc=1, device_id=(peer(dx, dz), ch), device_id_type=MESH)
    for d in range(1, CHAN):
        pl.semaphore_signal(barrier, inc=1, device_id=(me, lax.rem(ch + d, CHAN)), device_id_type=MESH)

    def block(j):
        return pl.ds(pl.multiple_of(j * CW, CW), CW)

    def channel_major(values, cb, dst):
        turned = jnp.transpose(values)
        for j in range(128 // CW):
            for h in range(PARTS):
                rows = slice(j * CW + h * CP, j * CW + h * CP + CP)
                both = jnp.concatenate([turned[rows, :BH], turned[rows, BH:]], axis=0)
                at = (cb * (128 // CW) + j) * CW
                dst[h, at : at + CW, :] = both.astype(bf16)

    loads[0].wait()
    loads[1].wait()
    for cb in range(CH // 128):
        lanes = slice(cb * 128, cb * 128 + 128)
        channel_major(k_ref[:, lanes].astype(f32) * v_ref[:, lanes].astype(f32), cb, prod_t)
    loads[2].wait()
    for g in range(8):
        taps_out[g] = taps_ref[g : g + 1, :].astype(f32)

    pl.semaphore_wait(barrier, SEQ - 1 + CHAN - 1)

    sends = []

    def exchange(src, dst, ssem, rsem):
        for dx, dz in order:
            j = peer(dx, dz)
            cp = pltpu.make_async_remote_copy(
                src.at[block(j)], dst.at[block(me)], ssem, rsem, device_id=(j, ch), device_id_type=MESH
            )
            cp.start()
            sends.append(cp)

    def arrived(dst, sem, count):
        pltpu.make_async_copy(dst.at[pl.ds(0, count)], dst.at[pl.ds(0, count)], sem).wait()

    exchange(prod_t.at[0], data_in.at[0], data_ssem.at[0], data_rsem.at[0])
    for dx, dz in order:
        j = peer(dx, dz)
        cp = pltpu.make_async_remote_copy(
            taps_out.at[j // 4], taps_in.at[me], taps_ssem, taps_rsem, device_id=(j, ch), device_id_type=MESH
        )
        cp.start()
        sends.append(cp)
    exchange(prod_t.at[1], data_in.at[1], data_ssem.at[1], data_rsem.at[1])
    taps_in[me] = taps_out[me // 4]
    for h in range(PARTS):
        data_in[h, block(me), :] = prod_t[h, block(me), :]

    loads[3].wait()
    for cb in range(CH // 128):
        lanes = slice(cb * 128, cb * 128 + 128)
        channel_major(q_ref[:, lanes].astype(f32), cb, q_t)

    for i in range(4, 8):
        loads[i].wait()
    arrived(taps_in, taps_rsem, SEQ - 1)
    for a in range(SEQ):
        taps_mat[a : a + 1, :] = taps_in[a]
    taps_y = jnp.dot(tfirst_ref[...], taps_mat[...].astype(bf16), preferred_element_type=f32)
    ty_re, ty_im = taps_y[:TPAD], taps_y[TPAD:]
    cos, sin = twid_ref[0], twid_ref[1]
    taps_spread = jnp.concatenate(
        [(ty_re * cos + ty_im * sin).astype(bf16), (ty_im * cos - ty_re * sin).astype(bf16)], axis=1
    )
    taps_spec[...] = jnp.dot(taps_spread, fwd[...], preferred_element_type=f32)
    loads[8].wait()
    loads[9].wait()

    zero = jnp.zeros((CP, BH), f32)

    def part(h):
        arrived(data_in.at[h], data_rsem.at[h], CH - CW)
        y = jnp.dot(first[...], data_in[h], preferred_element_type=f32)
        for bh in range(2):
            lanes = slice(bh * BH, bh * BH + BH)
            for m in range(ROWS // 16):
                res, ims = [], []
                for k1 in (2 * m, 2 * m + 1):
                    if k1 >= HALF:
                        res.append(zero)
                        ims.append(zero)
                        continue
                    at = k1 * CW + bh * CP
                    re = y[at : at + CP]
                    c = jnp.broadcast_to(twid_ref[0, k1 : k1 + 1, lanes], (CP, BH))
                    s = jnp.broadcast_to(twid_ref[1, k1 : k1 + 1, lanes], (CP, BH))
                    if 0 < k1 < HALF - 1:
                        at = (HALF + k1 - 1) * CW + bh * CP
                        im = y[at : at + CP]
                        res.append(re * c + im * s)
                        ims.append(im * c - re * s)
                    else:
                        res.append(re * c)
                        ims.append(-(re * s))
                rows = slice(m * 16, m * 16 + 16)
                spread[h, rows, lanes] = jnp.concatenate(res, axis=0).astype(bf16)
                spread[h, rows, slice(TOK + bh * BH, TOK + bh * BH + BH)] = jnp.concatenate(ims, axis=0).astype(bf16)

        for nb in range(TOK // 128):
            sp = jnp.dot(spread[h], fwd[:, nb * 256 : nb * 256 + 256], preferred_element_type=f32)
            lr, li = slice(nb * 256, nb * 256 + 128), slice(nb * 256 + 128, nb * 256 + 256)
            for m in range(ROWS // 16):
                res, ims = [], []
                for k1 in (2 * m, 2 * m + 1):
                    hr = jnp.broadcast_to(taps_spec[k1 : k1 + 1, lr], (CP, 128))
                    hi = jnp.broadcast_to(taps_spec[k1 : k1 + 1, li], (CP, 128))
                    rows = slice(k1 * CP, k1 * CP + CP)
                    sr, si = sp[rows, :128], sp[rows, 128:]
                    res.append(sr * hr - si * hi)
                    ims.append(sr * hi + si * hr)
                rows = slice(m * 16, m * 16 + 16)
                filtered[h, rows, lr] = jnp.concatenate(res, axis=0).astype(bf16)
                filtered[h, rows, li] = jnp.concatenate(ims, axis=0).astype(bf16)

        for nb in range(BH // 128):
            inv = jnp.dot(filtered[h], bwd[:, nb * 512 : nb * 512 + 512], preferred_element_type=f32)
            for k1 in range(HALF):
                rows = slice(k1 * CP, k1 * CP + CP)
                res, ims = [], []
                for bh in range(2):
                    lanes = slice(bh * BH + nb * 128, bh * BH + nb * 128 + 128)
                    c = jnp.broadcast_to(twid_ref[0, k1 : k1 + 1, lanes], (CP, 128))
                    s = jnp.broadcast_to(twid_ref[1, k1 : k1 + 1, lanes], (CP, 128))
                    re = inv[rows, bh * 256 : bh * 256 + 128]
                    im = inv[rows, bh * 256 + 128 : bh * 256 + 256]
                    res.append(re * c - im * s)
                    ims.append(im * c + re * s)
                lanes = slice(nb * 128, nb * 128 + 128)
                returned[h, k1 * CW : k1 * CW + CW, lanes] = jnp.concatenate(res, axis=0).astype(bf16)
                if 0 < k1 < HALF - 1:
                    at = (HALF + k1 - 1) * CW
                    returned[h, at : at + CW, lanes] = jnp.concatenate(ims, axis=0).astype(bf16)

        z = jnp.dot(last[...], returned[h], preferred_element_type=f32)
        back_out[h] = (z * (1.0 / N)).astype(bf16)
        exchange(back_out.at[h], back_in.at[h], back_ssem.at[h], back_rsem.at[h])
        back_in[h, block(me), :] = back_out[h, block(me), :]

    for h in range(PARTS):
        part(h)

    totals = [jnp.zeros((CP, BH), f32), jnp.zeros((CP, BH), f32)]
    for h in range(PARTS):
        arrived(back_in.at[h], back_rsem.at[h], CH - CW)
        for j in range(SEQ):
            rows = slice(j * CW, j * CW + CW)
            g = q_t[h, rows, :].astype(f32) * back_in[h, rows, :].astype(f32)
            g = g * g
            totals = [totals[0] + g[:CP], totals[1] + g[CP:]]
    for bh in range(2):
        sums_out[:, bh * BH : bh * BH + BH] = jnp.sum(totals[bh], axis=0, keepdims=True)
    for d in range(1, CHAN):
        cp = pltpu.make_async_remote_copy(
            sums_out, sums_in.at[ch], sum_ssem, sum_rsem, device_id=(me, lax.rem(ch + d, CHAN)), device_id_type=MESH
        )
        cp.start()
        sends.append(cp)
    sums_in[ch] = sums_out[...]

    for cb in range(CH // 128):
        rows = []
        for j in range(128 // CW):
            at = (cb * (128 // CW) + j) * CW
            for h in range(PARTS):
                tile = back_in[h, at : at + CW, :].astype(f32)
                rows.append(jnp.concatenate([tile[:CP], tile[CP:]], axis=1))
        conv[:, cb * 128 : cb * 128 + 128] = jnp.transpose(jnp.concatenate(rows, axis=0)).astype(bf16)
    conv_store = pltpu.make_async_copy(conv, conv_ref, load_sem.at[0])
    conv_store.start()

    arrived(sums_in, sum_rsem, CHAN - 1)
    square = sums_in[0]
    for i in range(1, CHAN):
        square = square + sums_in[i]
    inverse = lax.rsqrt(square / D + NORM_EPS)
    inverse_wide[...] = jnp.transpose(jnp.broadcast_to(inverse, (128, TOK)))
    inverse_store = pltpu.make_async_copy(inverse_wide, inverse_ref, load_sem.at[1])
    inverse_store.start()
    for cp in sends:
        cp.wait_send()
    conv_store.wait()
    inverse_store.wait()


def gate_and_norm(q_ref, conv_ref, inverse_ref, gain_ref, gated_ref, normed_ref):
    f32, bf16 = jnp.float32, jnp.bfloat16
    inverse = inverse_ref[...]
    for cb in range(CH // 128):
        lanes = slice(cb * 128, cb * 128 + 128)
        g = q_ref[:, lanes].astype(f32) * conv_ref[:, lanes].astype(f32)
        gated_ref[:, lanes] = g.astype(bf16)
        normed_ref[:, lanes] = (g * inverse * gain_ref[:, lanes]).astype(bf16)


def body(query_gate, key_gate, value_input, filter_taps, norm_gain):
    bf16, f32 = jnp.bfloat16, jnp.float32
    tables = [jnp.asarray(t) for t in constant_tables()]
    hbm = pl.BlockSpec(memory_space=pltpu.HBM)
    dma = pltpu.SemaphoreType.DMA
    conv, inverse = pl.pallas_call(
        kernel,
        out_shape=[jax.ShapeDtypeStruct((TOK, CH), bf16), jax.ShapeDtypeStruct((TOK, 128), f32)],
        in_specs=[hbm] * 10,
        out_specs=[hbm, hbm],
        scratch_shapes=[
            pltpu.VMEM((TOK, CH), bf16),
            pltpu.VMEM((TOK, CH), bf16),
            pltpu.VMEM((TOK, CH), bf16),
            pltpu.VMEM((8, TOK), bf16),
            pltpu.VMEM((2 * TPAD, SEQ), bf16),
            pltpu.VMEM((2, TPAD, TOK), f32),
            pltpu.VMEM((PARTS, CH, BH), bf16),
            pltpu.VMEM((PARTS, CH, BH), bf16),
            pltpu.VMEM((8, 1, TOK), f32),
            pltpu.VMEM((SEQ, 1, TOK), f32),
            pltpu.VMEM((SEQ, TOK), f32),
            pltpu.VMEM((TPAD, 2 * TOK), f32),
            pltpu.VMEM((PARTS, CH, BH), bf16),
            pltpu.VMEM((FULL, CH), bf16),
            pltpu.VMEM((CH, FULL), bf16),
            pltpu.VMEM((2 * TOK, 2 * TOK), bf16),
            pltpu.VMEM((2 * TOK, 2 * TOK), bf16),
            pltpu.VMEM((PARTS, ROWS, 2 * TOK), bf16),
            pltpu.VMEM((PARTS, ROWS, 2 * TOK), bf16),
            pltpu.VMEM((PARTS, FULL, BH), bf16),
            pltpu.VMEM((PARTS, CH, BH), bf16),
            pltpu.VMEM((PARTS, CH, BH), bf16),
            pltpu.VMEM((TOK, CH), bf16),
            pltpu.VMEM((TOK, 128), f32),
            pltpu.VMEM((1, TOK), f32),
            pltpu.VMEM((CHAN, 1, TOK), f32),
            dma((10,)), dma((PARTS,)), dma((PARTS,)), dma, dma, dma((PARTS,)), dma((PARTS,)), dma, dma,
        ],
        compiler_params=pltpu.CompilerParams(
            collective_id=0, has_side_effects=True, vmem_limit_bytes=56 * 1024 * 1024
        ),
    )(query_gate, key_gate, value_input, jnp.transpose(filter_taps), *tables)
    steps = 2
    wide = pl.BlockSpec((TOK // steps, CH), lambda i: (i, 0))
    return pl.pallas_call(
        gate_and_norm,
        grid=(steps,),
        out_shape=[jax.ShapeDtypeStruct((TOK, CH), bf16)] * 2,
        in_specs=[
            wide, wide, pl.BlockSpec((TOK // steps, 128), lambda i: (i, 0)), pl.BlockSpec((1, CH), lambda i: (0, 0))
        ],
        out_specs=[wide, wide],
        compiler_params=pltpu.CompilerParams(vmem_limit_bytes=56 * 1024 * 1024),
    )(query_gate, conv, inverse, norm_gain.reshape(1, CH))


def solution(mesh):
    placed = (P("seq", "chan"), P("seq", "chan"), P("seq", "chan"), P("seq", "chan"), P("chan"))
    return jax.shard_map(
        body,
        mesh=mesh,
        in_specs=placed,
        out_specs=(P("seq", "chan"), P("seq", "chan")),
        check_vma=False,
    )
```

time: 105 us -> 55.2 us (0.53)
  Pallas kernels: 0 us -> 54.4 us
  starting transfers between devices: 31.1 us -> 0 us
  other arithmetic: 20.4 us -> 0 us
  blocking collectives: 19.7 us -> 0 us
  waiting for transfers between devices: 17.6 us -> 0 us
  matrix products: 7.9 us -> 0 us
  local copies, waits for them, and re-layouts: 6.83 us -> 0 us
    pallas_call x0 -> x2, Pallas kernels: none -> 54.4 us  [the longest x1 52.2 us: body(): pl.pallas_call(kernel, out_shape=[jax.ShapeDtypeStruct((TOK, CH), bf16),...]
    all_to_all x3 -> x0, starting transfers between devices: 31.1 us -> none  [the longest x1 13.8 us: body(): lax.all_to_all(taps_major, 'seq', split_axis=0, concat_axis=1, tiled=True)]
    all_to_all x1 -> x0, blocking collectives: 19.7 us -> none  [from_everyone(): return lax.all_to_all(copies, axis, split_axis=0, concat_axis=0, tiled=True)]
    all_to_all x3 -> x0, waiting for transfers between devices: 17.6 us -> none  [the longest x1 12.7 us: body(): lax.all_to_all(local_blocks, 'seq', split_axis=1, concat_axis=0, tiled=True)]
    another operation x6 -> x0, other arithmetic: 15.3 us -> none
    dot_general x6 -> x0, matrix products: 7.9 us -> none  [the longest x2 4.14 us: spectrum_minor(): jnp.einsum('ckb,bm->ckm', joined, right_forward, preferred_element_type=j...]
    unnamed x23 -> x0, local copies, waits for them, and re-layouts: 4.38 us -> none
    convert_element_type x5 -> x0, other arithmetic: 3.12 us -> none  [the longest x2 1.31 us: spectrum_minor(): real_part.astype(jnp.bfloat16)]
  transfers between devices with their start and end apart: 3 -> 0, of which waited for: 2 -> 0; matrix products, arithmetic and copies ran while one was open for 20% -> 0% of each run, Pallas kernels for 0% -> 0%
where the time goes in v1:
time: 55.2 us; the launch traced here: 55 us
  Pallas kernels  54.4 us (99%)
  between operations  0.64 us (1%)
    pallas_call x1, Pallas kernels, body(): pl.pallas_call(kernel, out_shape=[jax.ShapeDtypeStruct((TOK, CH), bf16),...  52.2 us
    pallas_call x1, Pallas kernels, body(): pl.pallas_call(gate_and_norm, grid=(steps,), out_shape=[jax.ShapeDtypeStr...  2.2 us

profile of v1, /device:TPU:1, one launch (start us, length us, event | category | flops | bytes accessed | tf_op | source)
XLA Modules:
  0.0 55.0 jit_solution(13339506170730908175)
XLA Ops:
  0.6 52.2 %shard_map.122 = (bf16[512,512]{1,0:T(8,128)(2,1)}, f32[512,128]{1,0:T(8,128)}) custom-call(bf16[512,512]{1,0:T(8,128)(2,1)} %q_ref.1, bf16[512,512]{1,0:T(8,128)(2,1)} %k_hbm.1, bf16[512,512]{1,0:T(8,128)(2,1)} %v_hbm.1, bf16[8,512]{1,0:T(8,128)(2,1)} %bitcast.2, bf16[1024,512]{1,0:T(8,128)(2,1)} %constant.12.clone.first_hbm, ...), custom_call_target="tpu_custom_call" | custom-call | tf_op jit(solution)/shard_map/pallas_call | solution.py:322
  52.8 2.2 %shard_map.123 = (bf16[512,512]{1,0:T(8,128)(2,1)}, bf16[512,512]{1,0:T(8,128)(2,1)}) custom-call(bf16[512,512]{1,0:T(8,128)(2,1)} %q_ref.1, bf16[512,512]{1,0:T(8,128)(2,1)} %get-tuple-element.4.conv_ref, f32[512,128]{1,0:T(8,128)} %get-tuple-element.5.inverse_ref, f32[1,512]{1,0:T(1,128)} %bitcast.3), custom_call_target="tpu_custom_call" | custom-call | tf_op jit(solution)/shard_map/pallas_call | solution.py:362

commit v2 on v1

--- a/solution.py
+++ b/solution.py
@@ -77,11 +77,9 @@
 
 
 def send_order():
-    zs = (4, 3, 5, 2, 6, 1, 7, 0)
     out = []
-    for k in range(Z_DIM):
-        for dx in range(X_DIM):
-            dz = zs[(k + 2 * dx) % Z_DIM]
+    for dx in (1, 3, 2, 0):
+        for dz in (4, 3, 5, 2, 6, 1, 7, 0):
             if (dx, dz) != (0, 0):
                 out.append((dx, dz))
     return out
@@ -92,7 +90,7 @@
     conv_ref, inverse_ref,
     q_ref, k_ref, v_ref, taps_ref, tfirst_ref, twid_ref,
     prod_t, data_in, taps_out, taps_in, taps_mat, taps_spec, q_t,
-    first, last, fwd, bwd, spread, filtered, returned, back_out, back_in, conv, inverse_wide, sums_out, sums_in,
+    first, last, fwd, bwd, spread, filtered, returned, back_out, back_in, sums_out, sums_in,
     load_sem, data_ssem, data_rsem, taps_ssem, taps_rsem, back_ssem, back_rsem, sum_ssem, sum_rsem,
 ):
     f32, bf16 = jnp.float32, jnp.bfloat16
@@ -286,30 +284,26 @@
             for h in range(PARTS):
                 tile = back_in[h, at : at + CW, :].astype(f32)
                 rows.append(jnp.concatenate([tile[:CP], tile[CP:]], axis=1))
-        conv[:, cb * 128 : cb * 128 + 128] = jnp.transpose(jnp.concatenate(rows, axis=0)).astype(bf16)
-    conv_store = pltpu.make_async_copy(conv, conv_ref, load_sem.at[0])
-    conv_store.start()
+        conv_ref[:, cb * 128 : cb * 128 + 128] = jnp.transpose(jnp.concatenate(rows, axis=0)).astype(bf16)
 
     arrived(sums_in, sum_rsem, CHAN - 1)
     square = sums_in[0]
     for i in range(1, CHAN):
         square = square + sums_in[i]
     inverse = lax.rsqrt(square / D + NORM_EPS)
-    inverse_wide[...] = jnp.transpose(jnp.broadcast_to(inverse, (128, TOK)))
-    inverse_store = pltpu.make_async_copy(inverse_wide, inverse_ref, load_sem.at[1])
-    inverse_store.start()
+    inverse_ref[...] = jnp.transpose(jnp.broadcast_to(inverse, (128, TOK)))
     for cp in sends:
         cp.wait_send()
-    conv_store.wait()
-    inverse_store.wait()
 
 
 def gate_and_norm(q_ref, conv_ref, inverse_ref, gain_ref, gated_ref, normed_ref):
     f32, bf16 = jnp.float32, jnp.bfloat16
-    inverse = inverse_ref[...]
+    tokens = gated_ref.shape[0]
+    rows = pl.ds(pl.multiple_of(pl.program_id(0) * tokens, tokens), tokens)
+    inverse = inverse_ref[rows, :]
     for cb in range(CH // 128):
         lanes = slice(cb * 128, cb * 128 + 128)
-        g = q_ref[:, lanes].astype(f32) * conv_ref[:, lanes].astype(f32)
+        g = q_ref[rows, lanes].astype(f32) * conv_ref[rows, lanes].astype(f32)
         gated_ref[:, lanes] = g.astype(bf16)
         normed_ref[:, lanes] = (g * inverse * gain_ref[:, lanes]).astype(bf16)
 
@@ -319,11 +313,13 @@
     tables = [jnp.asarray(t) for t in constant_tables()]
     hbm = pl.BlockSpec(memory_space=pltpu.HBM)
     dma = pltpu.SemaphoreType.DMA
+    operands = [query_gate, key_gate, value_input, jnp.transpose(filter_taps), *tables]
+    vmem = pl.BlockSpec(memory_space=pltpu.VMEM)
     conv, inverse = pl.pallas_call(
         kernel,
-        out_shape=[jax.ShapeDtypeStruct((TOK, CH), bf16), jax.ShapeDtypeStruct((TOK, 128), f32)],
+        out_shape=[pltpu.VMEM((TOK, CH), bf16), pltpu.VMEM((TOK, 128), f32)],
         in_specs=[hbm] * 10,
-        out_specs=[hbm, hbm],
+        out_specs=[vmem, vmem],
         scratch_shapes=[
             pltpu.VMEM((TOK, CH), bf16),
             pltpu.VMEM((TOK, CH), bf16),
@@ -347,27 +343,23 @@
             pltpu.VMEM((PARTS, FULL, BH), bf16),
             pltpu.VMEM((PARTS, CH, BH), bf16),
             pltpu.VMEM((PARTS, CH, BH), bf16),
-            pltpu.VMEM((TOK, CH), bf16),
-            pltpu.VMEM((TOK, 128), f32),
             pltpu.VMEM((1, TOK), f32),
             pltpu.VMEM((CHAN, 1, TOK), f32),
             dma((10,)), dma((PARTS,)), dma((PARTS,)), dma, dma, dma((PARTS,)), dma((PARTS,)), dma, dma,
         ],
         compiler_params=pltpu.CompilerParams(
-            collective_id=0, has_side_effects=True, vmem_limit_bytes=56 * 1024 * 1024
+            collective_id=0, has_side_effects=True, vmem_limit_bytes=48 * 1024 * 1024
         ),
-    )(query_gate, key_gate, value_input, jnp.transpose(filter_taps), *tables)
-    steps = 2
+    )(*[pltpu.with_memory_space_constraint(x, pltpu.HBM) for x in operands])
+    steps = 4
     wide = pl.BlockSpec((TOK // steps, CH), lambda i: (i, 0))
     return pl.pallas_call(
         gate_and_norm,
         grid=(steps,),
         out_shape=[jax.ShapeDtypeStruct((TOK, CH), bf16)] * 2,
-        in_specs=[
-            wide, wide, pl.BlockSpec((TOK // steps, 128), lambda i: (i, 0)), pl.BlockSpec((1, CH), lambda i: (0, 0))
-        ],
+        in_specs=[vmem] * 4,
         out_specs=[wide, wide],
-        compiler_params=pltpu.CompilerParams(vmem_limit_bytes=56 * 1024 * 1024),
+        compiler_params=pltpu.CompilerParams(vmem_limit_bytes=32 * 1024 * 1024),
     )(query_gate, conv, inverse, norm_gain.reshape(1, CH))
 
 

time: 55.2 us -> 52.9 us (0.958)
  Pallas kernels: 54.4 us -> 52.1 us
    pallas_call x1, Pallas kernels: 52.2 us -> 50.5 us  [body(): pl.pallas_call(kernel, out_shape=[pltpu.VMEM((TOK, CH), bf16), pltpu.VMEM...]
    pallas_call x1, Pallas kernels: 2.2 us -> 1.63 us  [body(): pl.pallas_call(gate_and_norm, grid=(steps,), out_shape=[jax.ShapeDtypeStr...]
where the time goes in v2:
time: 52.9 us; the launch traced here: 52.8 us
  Pallas kernels  52.1 us (98%)
  between operations  0.67 us (1%)
    pallas_call x1, Pallas kernels, body(): pl.pallas_call(kernel, out_shape=[pltpu.VMEM((TOK, CH), bf16), pltpu.VMEM...  50.5 us
    pallas_call x1, Pallas kernels, body(): pl.pallas_call(gate_and_norm, grid=(steps,), out_shape=[jax.ShapeDtypeStr...  1.63 us

profile of v2, /device:TPU:1, one launch (start us, length us, event | category | flops | bytes accessed | tf_op | source)
XLA Modules:
  0.0 52.8 jit_solution(184491092482047311)
XLA Ops:
  0.6 0.0 copy-start
  0.6 0.0 copy-start.1
  0.7 50.5 %shard_map.122 = (bf16[512,512]{1,0:T(8,128)(2,1)S(1)}, f32[512,128]{1,0:T(8,128)S(1)}) custom-call(bf16[512,512]{1,0:T(8,128)(2,1)} %q_ref.1, bf16[512,512]{1,0:T(8,128)(2,1)} %k_hbm.1, bf16[512,512]{1,0:T(8,128)(2,1)} %v_hbm.1, bf16[8,512]{1,0:T(8,128)(2,1)} %bitcast.3, bf16[1024,512]{1,0:T(8,128)(2,1)} %constant.12.clone.first_hbm, ...), custom_call_target="tpu_custom_call" | custom-call | tf_op jit(solution)/shard_map/pallas_call | solution.py:318
  51.1 0.0 copy-done
  51.1 0.0 copy-done.1
  51.1 1.6 %shard_map.123 = (bf16[512,512]{1,0:T(8,128)(2,1)}, bf16[512,512]{1,0:T(8,128)(2,1)}) custom-call(bf16[512,512]{1,0:T(8,128)(2,1)S(1)} %copy-done, bf16[512,512]{1,0:T(8,128)(2,1)S(1)} %get-tuple-element.4.conv_ref, f32[512,128]{1,0:T(8,128)S(1)} %get-tuple-element.5.inverse_ref, f32[1,512]{1,0:T(1,128)S(1)} %bitcast.2), custom_call_target="tpu_custom_call" | custom-call | tf_op jit(solution)/shard_map/pallas_call | solution.py:356
Async XLA Ops:
  0.6 50.5 %copy-start = (bf16[512,512]{1,0:T(8,128)(2,1)S(1)}, bf16[512,512]{1,0:T(8,128)(2,1)}, u32[]{:S(2)}) copy-start(bf16[512,512]{1,0:T(8,128)(2,1)} %q_ref.1) | copy-start | bytes 1572868
  0.6 50.5 %copy-start.1 = (f32[512]{0:T(512)S(1)}, f32[512]{0:T(512)}, u32[]{:S(2)}) copy-start(f32[512]{0:T(512)} %param.15) | copy-start | bytes 6148

commit v3 on v2

--- a/solution.py
+++ b/solution.py
@@ -78,8 +78,8 @@
 
 def send_order():
     out = []
-    for dx in (1, 3, 2, 0):
-        for dz in (4, 3, 5, 2, 6, 1, 7, 0):
+    for dx in (2, 1, 3, 0):
+        for dz in (4, 1, 5, 2, 6, 3, 7, 0):
             if (dx, dz) != (0, 0):
                 out.append((dx, dz))
     return out
@@ -103,17 +103,18 @@
         (twid_hbm, twid_ref), (fwd_hbm, fwd), (first_hbm, first), (bwd_hbm, bwd), (last_hbm, last),
     ]
     loads = [pltpu.make_async_copy(src, dst, load_sem.at[i]) for i, (src, dst) in enumerate(loads)]
-    for load in loads:
+    for load in loads[:3]:
         load.start()
 
     def peer(dx, dz):
         return lax.rem(my_x + dx, X_DIM) * Z_DIM + lax.rem(my_z + dz, Z_DIM)
 
     order = send_order()
+    far_first = sorted(range(1, CHAN), key=lambda d: -min(d, CHAN - d))
     barrier = pltpu.get_barrier_semaphore()
     for dx, dz in order:
         pl.semaphore_signal(barrier, inc=1, device_id=(peer(dx, dz), ch), device_id_type=MESH)
-    for d in range(1, CHAN):
+    for d in far_first:
         pl.semaphore_signal(barrier, inc=1, device_id=(me, lax.rem(ch + d, CHAN)), device_id_type=MESH)
 
     def block(j):
@@ -130,6 +131,8 @@
 
     loads[0].wait()
     loads[1].wait()
+    for load in loads[3:]:
+        load.start()
     for cb in range(CH // 128):
         lanes = slice(cb * 128, cb * 128 + 128)
         channel_major(k_ref[:, lanes].astype(f32) * v_ref[:, lanes].astype(f32), cb, prod_t)
@@ -267,9 +270,12 @@
             g = q_t[h, rows, :].astype(f32) * back_in[h, rows, :].astype(f32)
             g = g * g
             totals = [totals[0] + g[:CP], totals[1] + g[CP:]]
-    for bh in range(2):
-        sums_out[:, bh * BH : bh * BH + BH] = jnp.sum(totals[bh], axis=0, keepdims=True)
-    for d in range(1, CHAN):
+    sums = [jnp.sum(t, axis=0, keepdims=True) for t in totals]
+    sums_out[...] = jnp.zeros((8, 128), f32)
+    for i in range(TOK // 128):
+        at = i * 128 % BH
+        sums_out[i : i + 1, :] = sums[i * 128 // BH][:, at : at + 128]
+    for d in far_first:
         cp = pltpu.make_async_remote_copy(
             sums_out, sums_in.at[ch], sum_ssem, sum_rsem, device_id=(me, lax.rem(ch + d, CHAN)), device_id_type=MESH
         )
@@ -291,7 +297,9 @@
     for i in range(1, CHAN):
         square = square + sums_in[i]
     inverse = lax.rsqrt(square / D + NORM_EPS)
-    inverse_ref[...] = jnp.transpose(jnp.broadcast_to(inverse, (128, TOK)))
+    for i in range(TOK // 128):
+        rows = slice(i * 128, i * 128 + 128)
+        inverse_ref[rows, :] = jnp.transpose(jnp.broadcast_to(inverse[i : i + 1, :], (128, 128)))
     for cp in sends:
         cp.wait_send()
 
@@ -343,15 +351,15 @@
             pltpu.VMEM((PARTS, FULL, BH), bf16),
             pltpu.VMEM((PARTS, CH, BH), bf16),
             pltpu.VMEM((PARTS, CH, BH), bf16),
-            pltpu.VMEM((1, TOK), f32),
-            pltpu.VMEM((CHAN, 1, TOK), f32),
+            pltpu.VMEM((8, 128), f32),
+            pltpu.VMEM((CHAN, 8, 128), f32),
             dma((10,)), dma((PARTS,)), dma((PARTS,)), dma, dma, dma((PARTS,)), dma((PARTS,)), dma, dma,
         ],
         compiler_params=pltpu.CompilerParams(
             collective_id=0, has_side_effects=True, vmem_limit_bytes=48 * 1024 * 1024
         ),
     )(*[pltpu.with_memory_space_constraint(x, pltpu.HBM) for x in operands])
-    steps = 4
+    steps = 2
     wide = pl.BlockSpec((TOK // steps, CH), lambda i: (i, 0))
     return pl.pallas_call(
         gate_and_norm,

time: 52.9 us -> 51.5 us (0.974)
  Pallas kernels: 52.1 us -> 50.7 us
    pallas_call x1, Pallas kernels: 50.5 us -> 49.6 us  [body(): pl.pallas_call(kernel, out_shape=[pltpu.VMEM((TOK, CH), bf16), pltpu.VMEM...]
where the time goes in v3:
time: 51.5 us; the launch traced here: 51.4 us
  Pallas kernels  50.7 us (98%)
  between operations  0.67 us (1%)
    pallas_call x1, Pallas kernels, body(): pl.pallas_call(kernel, out_shape=[pltpu.VMEM((TOK, CH), bf16), pltpu.VMEM...  49.6 us
    pallas_call x1, Pallas kernels, body(): pl.pallas_call(gate_and_norm, grid=(steps,), out_shape=[jax.ShapeDtypeStr...  1.1 us

profile of v3, /device:TPU:1, one launch (start us, length us, event | category | flops | bytes accessed | tf_op | source)
XLA Modules:
  0.0 51.4 jit_solution(2435171306221807224)
XLA Ops:
  0.6 0.0 copy-start
  0.6 0.0 copy-start.1
  0.7 49.6 %shard_map.122 = (bf16[512,512]{1,0:T(8,128)(2,1)S(1)}, f32[512,128]{1,0:T(8,128)S(1)}) custom-call(bf16[512,512]{1,0:T(8,128)(2,1)} %q_ref.1, bf16[512,512]{1,0:T(8,128)(2,1)} %k_hbm.1, bf16[512,512]{1,0:T(8,128)(2,1)} %v_hbm.1, bf16[8,512]{1,0:T(8,128)(2,1)} %bitcast.3, bf16[1024,512]{1,0:T(8,128)(2,1)} %constant.12.clone.first_hbm, ...), custom_call_target="tpu_custom_call" | custom-call | tf_op jit(solution)/shard_map/pallas_call | solution.py:326
  50.3 0.0 copy-done
  50.3 0.0 copy-done.1
  50.3 1.1 %shard_map.123 = (bf16[512,512]{1,0:T(8,128)(2,1)}, bf16[512,512]{1,0:T(8,128)(2,1)}) custom-call(bf16[512,512]{1,0:T(8,128)(2,1)S(1)} %copy-done, bf16[512,512]{1,0:T(8,128)(2,1)S(1)} %get-tuple-element.4.conv_ref, f32[512,128]{1,0:T(8,128)S(1)} %get-tuple-element.5.inverse_ref, f32[1,512]{1,0:T(1,128)S(1)} %bitcast.2), custom_call_target="tpu_custom_call" | custom-call | tf_op jit(solution)/shard_map/pallas_call | solution.py:364
Async XLA Ops:
  0.6 49.7 %copy-start = (bf16[512,512]{1,0:T(8,128)(2,1)S(1)}, bf16[512,512]{1,0:T(8,128)(2,1)}, u32[]{:S(2)}) copy-start(bf16[512,512]{1,0:T(8,128)(2,1)} %q_ref.1) | copy-start | bytes 1572868
  0.6 49.7 %copy-start.1 = (f32[512]{0:T(512)S(1)}, f32[512]{0:T(512)}, u32[]{:S(2)}) copy-start(f32[512]{0:T(512)} %param.15) | copy-start | bytes 6148
